TPU v7x, 32 devices: a whole 2x2x4 slice. The times are simulated.
32 devices in a mesh: band: 4 (over x, core), dom: 8 (over z, y).
Axes of the slice: x: 2, y: 2, z: 4, core: 2. Of those that a mesh axis runs over, the one named last changes fastest.
Arguments:
- orbitals: bfloat16 [20, 8, 8, 8, 4096], P(None, 'dom', None, None, 'band'), may hold values from -6 to 6
- rotation: bfloat16 [4096, 4096], P(None, 'band'), may hold values from -0.09375 to 0.09375
- potential: float32 [8, 8, 8, 8], P(None, 'dom'), may hold values from -4 to 4
Outputs:
- filtered: float32 [8, 8, 8, 8, 4096], P(None, 'dom', None, None, 'band')
All inputs are finite; a program needn't handle non-finite values.
Results may differ from a plain program's by a relative error of at most 0.0003.
Values may be sent and summed in bfloat16 or wider, within the bound.
A program may use at most 64 MiB of HBM per device.

v0:
```python
import jax
import jax.numpy as jnp
from jax import lax
from jax.sharding import PartitionSpec as P

TILES_Y = 4


stencil_weights = (
    -5369.0 / 1800.0,
    12.0 / 7.0,
    -15.0 / 56.0,
    10.0 / 189.0,
    -1.0 / 112.0,
    2.0 / 1925.0,
    -1.0 / 16632.0,
)
inverse_spacing = 4.0
centre_shift = 20.0
spread_scale = 24.0


def from_behind(value, axis, steps):
    count = lax.axis_size(axis)
    initial, last = (max(0, -steps), min(count, count - steps))
    return lax.ppermute(value, axis, [(source, source + steps) for source in range(initial, last)])


def apply_filter(slab_local, potential_local, fetch):
    reach = len(stencil_weights) - 1
    planes = potential_local.shape[0]
    extent_first = slab_local.shape[1]
    extent_second = slab_local.shape[2]
    middle = slab_local[reach : reach + planes]
    tile_row = lax.axis_index("dom") % TILES_Y
    below_first = fetch(middle[:, extent_first - reach :], TILES_Y)
    above_first = fetch(middle[:, :reach], -TILES_Y)
    below_second = fetch(middle[:, :, extent_second - reach :], 1)
    above_second = fetch(middle[:, :, :reach], -1)
    below_second = jnp.where(tile_row == 0, jnp.zeros_like(below_second), below_second)
    above_second = jnp.where(tile_row == TILES_Y - 1, jnp.zeros_like(above_second), above_second)
    widened_first = jnp.concatenate([below_first, middle, above_first], axis=1)
    widened_second = jnp.concatenate([below_second, middle, above_second], axis=2)
    accumulated = 3.0 * stencil_weights[0] * middle
    for offset in range(1, reach + 1):
        neighbours = slab_local[reach + offset : reach + offset + planes]
        neighbours = neighbours + slab_local[reach - offset : reach - offset + planes]
        neighbours = neighbours + widened_first[:, reach + offset : reach + offset + extent_first]
        neighbours = neighbours + widened_first[:, reach - offset : reach - offset + extent_first]
        neighbours = (
            neighbours + widened_second[:, :, reach + offset : reach + offset + extent_second]
        )
        neighbours = (
            neighbours + widened_second[:, :, reach - offset : reach - offset + extent_second]
        )
        accumulated = accumulated + stencil_weights[offset] * neighbours
    hamiltonian = (
        -0.5 * inverse_spacing * accumulated + (potential_local[..., None] - centre_shift) * middle
    )
    return hamiltonian / spread_scale


def on_device(orbitals, rotation, potential):
    ghosted = orbitals.shape[0]
    extent_first = orbitals.shape[2]
    extent_second = orbitals.shape[3]
    columns = orbitals.shape[4]
    planes = potential.shape[0]
    new_columns = rotation.shape[1]
    slab_local = orbitals.reshape(ghosted, extent_first, extent_second, columns)
    potential_local = potential.reshape(planes, extent_first, extent_second)
    flattened = slab_local.reshape(ghosted * extent_first * extent_second, columns)
    rotated = jnp.dot(
        lax.all_gather(flattened, "band", axis=1, tiled=True),
        rotation,
        preferred_element_type=jnp.float32,
    )
    rotated = rotated.reshape(ghosted, extent_first, extent_second, new_columns)

    def fetch_rotated(portion, distance):
        return from_behind(portion, "dom", distance)

    result = apply_filter(rotated, potential_local, fetch_rotated)
    return result.reshape(planes, 1, extent_first, extent_second, new_columns)


def solution(mesh):
    in_specs = (P(None, "dom", None, None, "band"), P(None, "band"), P(None, "dom", None, None))
    out_specs = P(None, "dom", None, None, "band")
    return jax.shard_map(
        on_device, mesh=mesh, in_specs=in_specs, out_specs=out_specs, check_vma=False
    )
```

profile of v0, /device:TPU:0, one launch (start us, length us, event | category | flops | bytes accessed | tf_op | source)
XLA Modules:
  0.0 249.7 jit_solution(14103050954694495129)
XLA Ops:
  6.5 0.0 all-gather.2.cloned.1.call-start
  6.5 0.7 all-gather.2.cloned.1.call-update
  7.3 74.6 %all-gather.2.cloned.1.call-done = bf16[1280,4096]{1,0:T(8,128)(2,1)} async-done(((bf16[1280,1024]{1,0:T(8,128)(2,1)}), bf16[1280,4096]{1,0:T(8,128)(2,1)}) %all-gather.2.cloned.1.call-update) | async-done | bytes 10485776 | tf_op jit(solution)/shard_map/all_gather | solution.py:74
  81.8 15.0 %fusion.62 = f32[1280,1024]{1,0:T(8,128)S(1)} fusion(bf16[1280,4096]{1,0:T(8,128)(2,1)} %all-gather.2.cloned.1.call-done, bf16[4096,1024]{1,0:T(8,128)(2,1)} %param.4), kind=kOutput, calls=%fused_computation.115 | convolution fusion | flops 10737418240 | bytes 24117248 | tf_op jit(solution)/shard_map/dot_general | solution.py:73
  96.8 5.2 %slice_add_fusion = (f32[512,1024]{1,0:T(8,128)}, f32[512,1024]{1,0:T(8,128)}, f32[512,1024]{1,0:T(8,128)}, f32[512,1024]{1,0:T(8,128)}, f32[512,1024]{1,0:T(8,1...) fusion(f32[1280,1024]{1,0:T(8,128)S(1)} %fusion.62), kind=kLoop, calls=%fused_computation.104 | loop fusion | flops 3145728 | bytes 41943040 | tf_op jit(solution)/shard_map/add | solution.py:47
  102.1 0.5 fusion.60
  102.6 2.1 copy.9
  104.6 4.5 %collective-permute-start.3 = (f32[8,8,6,1024]{3,1,2,0:T(8,128)}, f32[8,8,6,1024]{3,1,2,0:T(8,128)}, u32[]{:S(2)}, u32[]{:S(2)}) collective-permute-start(f32[8,8,6,1024]{3,1,2,0:T(8,128)} %copy.9), channel_id=1, source_target_pairs={{0,1},{1,2},{2,3},{3,4},{4,5},{5,6},{6,7},{8,9},{9,10},{10,11},{11... | collective-permute-start | bytes 4718600 | tf_op jit(solution)/shard_map/ppermute | solution.py:26
  109.2 2.1 copy.8
  111.2 0.0 copy-start
  111.2 1.4 collective-permute-start.2
  112.7 2.1 fusion.61
  114.7 1.3 collective-permute-start
  116.0 7.8 %collective-permute-start.1 = (f32[8,6,8,1024]{3,2,1,0:T(8,128)}, f32[8,6,8,1024]{3,2,1,0:T(8,128)}, u32[]{:S(2)}, u32[]{:S(2)}) collective-permute-start(f32[8,6,8,1024]{3,2,1,0:T(8,128)} %get-tuple-element.15), channel_id=1, source_target_pairs={{0,4},{1,5},{2,6},{3,7},{8,12},{9,13},{10,14},{11,15},{16,20},{17,... | collective-permute-start | bytes 4718600 | tf_op jit(solution)/shard_map/ppermute | solution.py:26
  123.8 0.0 copy-done
  123.8 52.3 %collective-permute-done.3 = f32[8,8,6,1024]{3,1,2,0:T(8,128)} collective-permute-done((f32[8,8,6,1024]{3,1,2,0:T(8,128)}, f32[8,8,6,1024]{3,1,2,0:T(8,128)}, u32[]{:S(2)}, u32[]{:S(2)}) %collective-permute-start.3) | collective-permute-done | bytes 1572896 | tf_op jit(solution)/shard_map/ppermute | solution.py:26
  176.1 0.2 broadcast_select_fusion
  176.3 2.3 copy.7
  178.5 0.0 collective-permute-done.2
  178.5 1.6 broadcast_select_fusion.1
  180.1 2.2 copy.5
  182.4 35.6 %collective-permute-done = f32[8,6,8,1024]{3,2,1,0:T(8,128)} collective-permute-done((f32[8,6,8,1024]{3,2,1,0:T(8,128)}, f32[8,6,8,1024]{3,2,1,0:T(8,128)}, u32[]{:S(2)}, u32[]{:S(2)}) %collective-permute-start) | collective-permute-done | bytes 1572896 | tf_op jit(solution)/shard_map/ppermute | solution.py:26
  218.0 0.0 collective-permute-done.1
  218.0 24.8 %fusion.10 = f32[8,1,8,8,1024]{4,3,2,1,0:T(8,128)} fusion(f32[8,8,8,1024]{3,2,1,0:T(8,128)S(1)} %bitcast.16, f32[8,8,8,1024]{3,2,1,0:T(8,128)} %bitcast.22, f32[8,8,8,1024]{3,2,1,0:T(8,128)} %bitcast.21, f32[8,8,8,1024]{3,2,1,0:T(8,128)} %bitcast.19, f32[8,8,8,1024]{3,2,1,0:T(8,128)} %bitcast.18, f32[8,8,8,1024]{3,2,1,0:T(8,128)} %bitcast.20, ...), kind=kLoop, calls=%fused_computation.50 | loop fusion | flops 34078720 | bytes 23070720 | tf_op jit(solution)/shard_map/reshape | solution.py:84
  (1 shorter events, 0.0 us)
Async XLA Ops:
  6.5 75.3 %all-gather.2.cloned.1.call-start = ((), (), s32[]{:S(2)}) async-start(), calls=%async_computation | async-start | bytes 13107200 | tf_op jit(solution)/shard_map/all_gather | solution.py:74
  104.6 71.5 %collective-permute-start.3 = (f32[8,8,6,1024]{3,1,2,0:T(8,128)}, f32[8,8,6,1024]{3,1,2,0:T(8,128)}, u32[]{:S(2)}, u32[]{:S(2)}) collective-permute-start(f32[8,8,6,1024]{3,1,2,0:T(8,128)} %copy.9), channel_id=1, source_target_pairs={{0,1},{1,2},{2,3},{3,4},{4,5},{5,6},{6,7},{8,9},{9,10},{10,11},{11... | collective-permute-start | bytes 4718600 | tf_op jit(solution)/shard_map/ppermute | solution.py:26
  111.2 12.5 %copy-start = (f32[8,1,8,8]{3,2,1,0:T(8,128)S(1)}, f32[8,1,8,8]{3,2,1,0:T(8,128)}, u32[]{:S(2)}) copy-start(f32[8,1,8,8]{3,2,1,0:T(8,128)} %param.5) | copy-start | bytes 6148
  111.2 67.3 %collective-permute-start.2 = (f32[8,8,6,1024]{3,1,2,0:T(8,128)}, f32[8,8,6,1024]{3,1,2,0:T(8,128)}, u32[]{:S(2)}, u32[]{:S(2)}) collective-permute-start(f32[8,8,6,1024]{3,1,2,0:T(8,128)} %copy.8), channel_id=1, source_target_pairs={{1,0},{2,1},{3,2},{4,3},{5,4},{6,5},{7,6},{9,8},{10,9},{11,10},{12... | collective-permute-start | bytes 4718600 | tf_op jit(solution)/shard_map/ppermute | solution.py:26
  114.7 103.2 %collective-permute-start = (f32[8,6,8,1024]{3,2,1,0:T(8,128)}, f32[8,6,8,1024]{3,2,1,0:T(8,128)}, u32[]{:S(2)}, u32[]{:S(2)}) collective-permute-start(f32[8,6,8,1024]{3,2,1,0:T(8,128)} %get-tuple-element.14), channel_id=1, source_target_pairs={{4,0},{5,1},{6,2},{7,3},{12,8},{13,9},{14,10},{15,11},{20,16},{21,... | collective-permute-start | bytes 4718600 | tf_op jit(solution)/shard_map/ppermute | solution.py:26
  116.0 102.0 %collective-permute-start.1 = (f32[8,6,8,1024]{3,2,1,0:T(8,128)}, f32[8,6,8,1024]{3,2,1,0:T(8,128)}, u32[]{:S(2)}, u32[]{:S(2)}) collective-permute-start(f32[8,6,8,1024]{3,2,1,0:T(8,128)} %get-tuple-element.15), channel_id=1, source_target_pairs={{0,4},{1,5},{2,6},{3,7},{8,12},{9,13},{10,14},{11,15},{16,20},{17,... | collective-permute-start | bytes 4718600 | tf_op jit(solution)/shard_map/ppermute | solution.py:26
Sparse Core Ops, SparseCore 0:
  8.9 72.8 all-gather.1
where the time goes:
time: 250 us
  waiting for transfers between devices  163 us (65%)
  other arithmetic  31.8 us (13%)
  starting transfers between devices  15 us (6%)
  matrix products  15 us (6%)
  between operations  13.5 us (5%)
  local copies, waits for them, and re-layouts  11.2 us (4%)
    ppermute x4, waiting for transfers between devices, from_behind(): lax.ppermute(value, axis, [(source, source + steps) for source in range(i...  88 us
    all_gather x1, waiting for transfers between devices, on_device(): lax.all_gather(flattened, 'band', axis=1, tiled=True)  74.6 us
    reshape x1, other arithmetic, on_device(): return result.reshape(planes, 1, extent_first, extent_second, new_columns)  24.8 us
    dot_general x1, matrix products, on_device(): jnp.dot(lax.all_gather(flattened, 'band', axis=1, tiled=True), rotation,...  15 us
    ppermute x4, starting transfers between devices, from_behind(): lax.ppermute(value, axis, [(source, source + steps) for source in range(i...  15 us
    add x1, other arithmetic, apply_filter(): neighbours = neighbours + slab_local[reach - offset:reach - offset + planes]  5.23 us
  transfers between devices with their start and end apart: 5, of which 3 were waited for; matrix products, arithmetic and copies ran while one was open for 4% of the time, Pallas kernels for 0%

commit v1 on v0

v1 whole, which is shorter than its diff:
```python
import functools

import jax
import jax.numpy as jnp
import numpy as np
from jax import lax
from jax.experimental import pallas as pl
from jax.experimental.pallas import tpu as pltpu
from jax.sharding import PartitionSpec as P

TILES_Y = 4
MESH = pl.DeviceIdType.MESH

stencil_weights = (
    -5369.0 / 1800.0,
    12.0 / 7.0,
    -15.0 / 56.0,
    10.0 / 189.0,
    -1.0 / 112.0,
    2.0 / 1925.0,
    -1.0 / 16632.0,
)
inverse_spacing = 4.0
centre_shift = 20.0
spread_scale = 24.0
REACH = len(stencil_weights) - 1
FACTOR = -0.5 * inverse_spacing / spread_scale
PEAK = 2.0**15
LANES = 128


def three_parts(matrix):
    rest = jnp.asarray(matrix, jnp.float32)
    pieces = []
    for _ in range(3):
        piece = rest.astype(jnp.bfloat16)
        pieces.append(piece)
        rest = rest - piece.astype(jnp.float32)
    return jnp.concatenate(pieces, axis=0)


def plane_matrices(ex, ey):
    def weight(x0, y0, x1, y1):
        dx, dy = abs(x0 - x1), abs(y0 - y1)
        if (dx == 0) == (dy == 0) or dx + dy > REACH:
            return 0.0
        return FACTOR * stencil_weights[dx + dy]

    points = [(x, y) for x in range(ex) for y in range(ey)]
    halo = [(x - REACH, y) for x in range(REACH) for y in range(ey)]
    halo += [(ex + x, y) for x in range(REACH) for y in range(ey)]
    halo += [(x, y - REACH) for x in range(ex) for y in range(REACH)]
    halo += [(x, ey + y) for x in range(ex) for y in range(REACH)]
    own = np.array([[weight(*a, *b) for b in points] for a in points], np.float32)
    outer = np.array([[weight(*a, *b) for b in halo] for a in points], np.float32)
    pick = [(x, ey - REACH + y) for x in range(ex) for y in range(REACH)]
    pick += [(x, y) for x in range(ex) for y in range(REACH)]
    select = np.array([[float(a == b) for b in points] for a in pick], np.float32)
    return own, outer, select


def kernel(
    bands, doms, ex, ey,
    orb_hbm, rot_hbm, centre_ref, own_ref, outer_ref, select_ref, out_hbm,
    orb, rot, halo, packed, part, code, lhs, result,
    load_sem, halo_send, halo_recv, code_send, code_recv, forward_send, out_sem,
):
    planes = part.shape[0]
    points = part.shape[1]
    cols = part.shape[2]
    step = min(cols, 256)
    along_x, along_y = REACH * ey, REACH * ex
    peers = bands // 2
    band, dom = lax.axis_index("band"), lax.axis_index("dom")
    sibling = band + 1 - 2 * lax.rem(band, 2)
    row = lax.rem(dom, TILES_Y)
    starts = (0, along_x, 2 * along_x, 2 * along_x + along_y)
    sizes = (along_x, along_x, along_y, along_y)
    distance = (-TILES_Y, TILES_Y, -1, 1)
    has = (dom >= TILES_Y, dom < doms - TILES_Y, row > 0, row < TILES_Y - 1)

    def cyc(first, j):
        return lax.rem(first + 2 * j, bands)

    load_orb = pltpu.make_async_copy(orb_hbm, orb, load_sem.at[0])
    load_rot = pltpu.make_async_copy(rot_hbm, rot, load_sem.at[1])
    load_orb.start()
    load_rot.start()

    barrier = pltpu.get_barrier_semaphore()
    for k in range(4):
        @pl.when(has[k])
        def _():
            pl.semaphore_signal(
                barrier, inc=1, device_id=(band, dom + distance[k]), device_id_type=MESH
            )
    for j in range(1, peers):
        pl.semaphore_signal(barrier, inc=1, device_id=(cyc(band, j), dom), device_id_type=MESH)
    pl.semaphore_signal(barrier, inc=1, device_id=(sibling, dom), device_id_type=MESH)
    for k in range(4):
        @pl.when(jnp.logical_not(has[k]))
        def _():
            halo[:, starts[k] : starts[k] + sizes[k], :] = jnp.zeros(
                (planes, sizes[k], cols), halo.dtype
            )
    load_orb.wait()
    there = peers
    for k in range(4):
        there = there + has[k].astype(jnp.int32)
    pl.semaphore_wait(barrier, there)

    def halo_copy(k, p):
        source = (
            orb.at[REACH + p, pl.ds(points - along_x, along_x)],
            orb.at[REACH + p, pl.ds(0, along_x)],
            packed.at[p, pl.ds(0, along_y)],
            packed.at[p, pl.ds(along_y, along_y)],
        )[k]
        return pltpu.make_async_remote_copy(
            src_ref=source,
            dst_ref=halo.at[p, pl.ds(starts[k], sizes[k])],
            send_sem=halo_send.at[k, p],
            recv_sem=halo_recv.at[k, p],
            device_id=(band, dom - distance[k]),
            device_id_type=MESH,
        )

    def sends(k):
        return has[k ^ 1]

    def code_copy(source, p, target, send_sem):
        return pltpu.make_async_remote_copy(
            src_ref=code.at[source, p],
            dst_ref=code.at[source, p],
            send_sem=send_sem,
            recv_sem=code_recv.at[source, p],
            device_id=(target, dom),
            device_id_type=MESH,
        )

    @pl.loop(0, planes)
    def _(p):
        for k in (0, 1):
            @pl.when(sends(k))
            def _():
                halo_copy(k, p).start()
        for n in range(0, cols, step):
            packed[p, :, n : n + step] = jnp.dot(
                select_ref[...], orb[REACH + p, :, n : n + step],
                preferred_element_type=jnp.float32,
            ).astype(packed.dtype)
        for k in (2, 3):
            @pl.when(sends(k))
            def _():
                halo_copy(k, p).start()

    def three_sum(value):
        return value[:points] + value[points : 2 * points] + value[2 * points :]

    @pl.loop(0, planes)
    def _(p):
        for n in range(0, cols, step):
            at = slice(n, n + step)
            total = three_sum(
                jnp.dot(
                    own_ref[...], orb[REACH + p, :, at], preferred_element_type=jnp.float32
                )
            )
            for k in range(1, REACH + 1):
                pair = orb[REACH + p + k, :, at].astype(jnp.float32)
                pair = pair + orb[REACH + p - k, :, at].astype(jnp.float32)
                total = total + (FACTOR * stencil_weights[k]) * pair
            total = total + centre_ref[p, :, 0:1] * orb[REACH + p, :, at].astype(jnp.float32)
            part[p, :, at] = total

    load_rot.wait()

    def filter_plane(p):
        for k in range(4):
            @pl.when(has[k])
            def _():
                halo_copy(k, p).wait_recv()
        largest = jnp.zeros((points, 1), jnp.float32)
        for n in range(0, cols, step):
            at = slice(n, n + step)
            total = part[p, :, at] + three_sum(
                jnp.dot(outer_ref[...], halo[p, :, at], preferred_element_type=jnp.float32)
            )
            part[p, :, at] = total
            largest = jnp.maximum(largest, jnp.max(jnp.abs(total), axis=1, keepdims=True))
        scale = jnp.maximum(largest, 1e-30).astype(code.dtype)
        code[band, p, :, cols:] = jnp.broadcast_to(scale, (points, LANES))
        inverse = PEAK / scale.astype(jnp.float32)
        for n in range(0, cols, step):
            at = slice(n, n + step)
            x = part[p, :, at] * inverse
            y = x * x
            y = y * y
            y = y * y
            code[band, p, :, at] = jnp.where(x < 0, -y, y).astype(code.dtype)
        for j in range(1, peers):
            code_copy(band, p, cyc(band, j), code_send.at[j, p]).start()
        code_copy(band, p, sibling, forward_send.at[0, p]).start()

    def forward(p):
        for j in range(1, peers):
            source = cyc(band, j)
            code_copy(source, p, sibling, code_send.at[j, p]).wait_recv()
            code_copy(source, p, sibling, forward_send.at[j, p]).start()

    def split(slot, at, value):
        high = value.astype(lhs.dtype)
        lhs[slot, :points, at] = high
        lhs[slot, points:, at] = (value - high.astype(jnp.float32)).astype(lhs.dtype)

    def decode(source, p):
        shift = jnp.log2(code[source, p, :, cols : cols + 1].astype(jnp.float32) * (1.0 / PEAK))
        for n in range(0, cols, step):
            at = slice(n, n + step)
            y = code[source, p, :, at].astype(jnp.float32)
            size = jnp.exp2(jnp.log2(jnp.abs(y)) * 0.125 + shift)
            split(source, at, jnp.where(y < 0, -size, size))

    def rotate(p):
        for n in range(0, cols, step):
            at = slice(n, n + step)
            split(band, at, part[p, :, at])
        for j in range(1, peers):
            decode(cyc(band, j), p)
        for j in range(peers):
            source = cyc(sibling, j)
            code_copy(source, p, sibling, code_send.at[0, p]).wait_recv()
            decode(source, p)
        for n in range(0, cols, step):
            at = slice(n, n + step)
            total = jnp.zeros((2 * points, step), jnp.float32)
            for s in range(bands):
                total = total + jnp.dot(
                    lhs[s], rot[s * cols : (s + 1) * cols, at],
                    preferred_element_type=jnp.float32,
                )
            result[p, :, at] = total[:points] + total[points:]
        pltpu.make_async_copy(result.at[p], out_hbm.at[p], out_sem.at[p]).start()

    @pl.loop(0, planes + 2)
    def _(p):
        @pl.when(p < planes)
        def _():
            filter_plane(p)

        @pl.when(p >= 2)
        def _():
            rotate(p - 2)

        @pl.when(jnp.logical_and(p >= 1, p <= planes))
        def _():
            forward(p - 1)

    @pl.loop(0, planes)
    def _(p):
        for k in range(4):
            @pl.when(sends(k))
            def _():
                halo_copy(k, p).wait_send()
        for j in range(1, peers):
            code_copy(band, p, cyc(band, j), code_send.at[j, p]).wait_send()
        for j in range(peers):
            code_copy(cyc(band, j), p, sibling, forward_send.at[j, p]).wait_send()
        pltpu.make_async_copy(result.at[p], out_hbm.at[p], out_sem.at[p]).wait()


def on_device(orbitals, rotation, potential):
    ghosted, _, ex, ey, cols = orbitals.shape
    planes = potential.shape[0]
    points = ex * ey
    new_cols = rotation.shape[1]
    bands, doms = lax.axis_size("band"), lax.axis_size("dom")
    own, outer, select = plane_matrices(ex, ey)
    centre = (
        3.0 * stencil_weights[0] * -0.5 * inverse_spacing
        + (potential.reshape(planes, points, 1) - centre_shift)
    ) / spread_scale
    bf16, f32 = jnp.bfloat16, jnp.float32
    dma = pltpu.SemaphoreType.DMA
    whole = pl.BlockSpec(memory_space=pltpu.VMEM)
    away = pl.BlockSpec(memory_space=pl.ANY)
    result = pl.pallas_call(
        functools.partial(kernel, bands, doms, ex, ey),
        out_shape=jax.ShapeDtypeStruct((planes, points, new_cols), f32),
        in_specs=[away, away, whole, whole, whole, whole],
        out_specs=away,
        scratch_shapes=[
            pltpu.VMEM((ghosted, points, cols), bf16),
            pltpu.VMEM(rotation.shape, bf16),
            pltpu.VMEM((planes, outer.shape[1], cols), bf16),
            pltpu.VMEM((planes, select.shape[0], cols), bf16),
            pltpu.VMEM((planes, points, cols), f32),
            pltpu.VMEM((bands, planes, points, cols + LANES), bf16),
            pltpu.VMEM((bands, 2 * points, cols), bf16),
            pltpu.VMEM((planes, points, new_cols), f32),
            dma((2,)),
            dma((4, planes)),
            dma((4, planes)),
            dma((bands // 2, planes)),
            dma((bands, planes)),
            dma((bands // 2, planes)),
            dma((planes,)),
        ],
        compiler_params=pltpu.CompilerParams(
            collective_id=0, has_side_effects=True, vmem_limit_bytes=50 * 2**20
        ),
        cost_estimate=pl.CostEstimate(
            flops=4 * planes * points * cols * bands * new_cols,
            bytes_accessed=2 * (orbitals.size + rotation.size) + 4 * planes * points * new_cols,
            transcendentals=0,
        ),
    )(
        orbitals.reshape(ghosted, points, cols),
        rotation,
        centre,
        three_parts(own),
        three_parts(outer),
        jnp.asarray(select, bf16),
    )
    return result.reshape(planes, 1, ex, ey, new_cols)


def solution(mesh):
    in_specs = (P(None, "dom", None, None, "band"), P(None, "band"), P(None, "dom", None, None))
    out_specs = P(None, "dom", None, None, "band")
    return jax.shard_map(
        on_device, mesh=mesh, in_specs=in_specs, out_specs=out_specs, check_vma=False
    )
```

time: 250 us -> 61.1 us (0.24)
  the two profiles are of different devices: /device:TPU:0 before, /device:TPU:5 now
where the time goes in v1:
time: 61.1 us; the launch traced here: 60.8 us
  Pallas kernels  56.1 us (92%)
  local copies, waits for them, and re-layouts  3.87 us (6%)
  other arithmetic  0.76 us (1%)
    pallas_call x1, Pallas kernels, on_device(): pl.pallas_call(functools.partial(kernel, bands, doms, ex, ey), out_shape=...  56.1 us
    unnamed x7, local copies, waits for them, and re-layouts  3.74 us

profile of v1, /device:TPU:5, one launch (start us, length us, event | category | flops | bytes accessed | tf_op | source)
XLA Modules:
  0.0 60.8 jit_solution(1394406038402444722)
XLA Ops:
  0.0 0.8 %add_multiply_fusion = f32[8,1,8,8]{3,2,1,0:T(8,128)S(1)} fusion(f32[8,1,8,8]{3,2,1,0:T(8,128)} %param.8), kind=kLoop, calls=%fused_computation | loop fusion | flops 1024 | bytes 4096 | tf_op jit(solution)/shard_map/div | solution.py:279
  0.8 0.1 div.11.centre_ref
  0.9 0.0 copy-start
  0.9 0.9 %copy-done = bf16[192,192]{1,0:T(8,128)(2,1)S(1)} copy-done((bf16[192,192]{1,0:T(8,128)(2,1)S(1)}, bf16[192,192]{1,0:T(8,128)(2,1)}, u32[]{:S(2)}) %copy-start) | copy-done | bytes 73752
  1.8 0.0 copy-start.1
  1.8 0.8 %copy-done.1 = bf16[192,64]{1,0:T(8,128)(2,1)S(1)} copy-done((bf16[192,64]{1,0:T(8,128)(2,1)S(1)}, bf16[192,64]{1,0:T(8,128)(2,1)}, u32[]{:S(2)}) %copy-start.1) | copy-done | bytes 24600
  2.6 0.0 copy-start.2
  2.6 0.7 %copy-done.2 = bf16[96,64]{1,0:T(8,128)(2,1)S(1)} copy-done((bf16[96,64]{1,0:T(8,128)(2,1)S(1)}, bf16[96,64]{1,0:T(8,128)(2,1)}, u32[]{:S(2)}) %copy-start.2) | copy-done | bytes 12312
  3.3 56.1 %shard_map.64 = f32[8,64,1024]{2,1,0:T(8,128)S(1)} custom-call(bf16[20,64,1024]{2,1,0:T(8,128)(2,1)} %bitcast.7, bf16[4096,1024]{1,0:T(8,128)(2,1)} %rot_hbm.1, f32[8,64,1]{2,1,0:T(8,128)S(1)} %div.11.centre_ref, bf16[192,64]{1,0:T(8,128)(2,1)S(1)} %copy-done.1, bf16[192,192]{1,0:T(8,128)(2,1)S(1)} %copy-done, bf16[96,64]{1,0:T(8,128)(2,1)S(1)} %copy-done.2), custom_call_target="tpu_custom_call" | custom-call | flops 8589934592 | bytes 13107200 | tf_op jit(solution)/shard_map/pallas_call | solution.py:287
  59.4 1.3 %copy.11 = f32[8,1,8,8,1024]{4,3,2,1,0:T(8,128)} copy(f32[8,1,8,8,1024]{4,3,2,1,0:T(8,128)S(1)} %bitcast.6) | data formatting | bytes 4194304
Async XLA Ops:
  0.9 0.9 %copy-start = (bf16[192,192]{1,0:T(8,128)(2,1)S(1)}, bf16[192,192]{1,0:T(8,128)(2,1)}, u32[]{:S(2)}) copy-start(bf16[192,192]{1,0:T(8,128)(2,1)} %constant.34.outer_ref) | copy-start | bytes 221188
  1.8 0.8 %copy-start.1 = (bf16[192,64]{1,0:T(8,128)(2,1)S(1)}, bf16[192,64]{1,0:T(8,128)(2,1)}, u32[]{:S(2)}) copy-start(bf16[192,64]{1,0:T(8,128)(2,1)} %constant.26.own_ref) | copy-start | bytes 73732
  2.6 0.7 %copy-start.2 = (bf16[96,64]{1,0:T(8,128)(2,1)S(1)}, bf16[96,64]{1,0:T(8,128)(2,1)}, u32[]{:S(2)}) copy-start(bf16[96,64]{1,0:T(8,128)(2,1)} %constant.16.clone.select_ref) | copy-start | bytes 36868

commit v2 on v1

--- a/solution.py
+++ b/solution.py
@@ -26,43 +26,69 @@
 REACH = len(stencil_weights) - 1
 FACTOR = -0.5 * inverse_spacing / spread_scale
 PEAK = 2.0**15
+AHEAD = 2
 LANES = 128
 
 
-def three_parts(matrix):
-    rest = jnp.asarray(matrix, jnp.float32)
+def divide(value, by):
+    if by & (by - 1) == 0:
+        return value >> (by.bit_length() - 1), value & (by - 1)
+    return value // by, value % by
+
+
+def weight_parts():
     pieces = []
-    for _ in range(3):
-        piece = rest.astype(jnp.bfloat16)
-        pieces.append(piece)
-        rest = rest - piece.astype(jnp.float32)
-    return jnp.concatenate(pieces, axis=0)
-
-
-def plane_matrices(ex, ey):
-    def weight(x0, y0, x1, y1):
-        dx, dy = abs(x0 - x1), abs(y0 - y1)
-        if (dx == 0) == (dy == 0) or dx + dy > REACH:
-            return 0.0
-        return FACTOR * stencil_weights[dx + dy]
-
-    points = [(x, y) for x in range(ex) for y in range(ey)]
-    halo = [(x - REACH, y) for x in range(REACH) for y in range(ey)]
-    halo += [(ex + x, y) for x in range(REACH) for y in range(ey)]
-    halo += [(x, y - REACH) for x in range(ex) for y in range(REACH)]
-    halo += [(x, ey + y) for x in range(ex) for y in range(REACH)]
-    own = np.array([[weight(*a, *b) for b in points] for a in points], np.float32)
-    outer = np.array([[weight(*a, *b) for b in halo] for a in points], np.float32)
-    pick = [(x, ey - REACH + y) for x in range(ex) for y in range(REACH)]
-    pick += [(x, y) for x in range(ex) for y in range(REACH)]
-    select = np.array([[float(a == b) for b in points] for a in pick], np.float32)
-    return own, outer, select
+    for weight in stencil_weights[1:]:
+        rest, three = np.float32(FACTOR * weight), []
+        for _ in range(3):
+            piece = np.float32(rest.astype(jnp.bfloat16))
+            three.append(float(piece))
+            rest = np.float32(rest - piece)
+        pieces.append(three)
+    return pieces
+
+
+def fill_matrices(own, outer, select, ex, ey):
+    points = ex * ey
+    along_x, along_y = REACH * ey, REACH * ex
+    pieces = weight_parts()
+
+    def fill(ref, x0, y0, x1, y1):
+        dx, dy = jnp.abs(x0 - x1), jnp.abs(y0 - y1)
+        reach = jnp.where(dx == 0, dy, jnp.where(dy == 0, dx, 0))
+        for part in range(3):
+            value = jnp.zeros(reach.shape, jnp.float32)
+            for k in range(1, REACH + 1):
+                value = jnp.where(reach == k, pieces[k - 1][part], value)
+            ref[part * points : (part + 1) * points, :] = value.astype(ref.dtype)
+
+    def grid(shape):
+        return lax.broadcasted_iota(jnp.int32, shape, 0), lax.broadcasted_iota(jnp.int32, shape, 1)
+
+    r, c = grid((points, points))
+    fill(own, *divide(r, ey), *divide(c, ey))
+    r, c = grid((points, 2 * (along_x + along_y)))
+    in_x = c < 2 * along_x
+    second = (in_x & (c >= along_x)) | (c >= 2 * along_x + along_y)
+    at_x = jnp.where(c >= along_x, c - along_x, c)
+    at_y = jnp.maximum(c - 2 * along_x, 0)
+    at_y = jnp.where(at_y >= along_y, at_y - along_y, at_y)
+    far_x, near_y = divide(at_x, ey)
+    far_y, near_x = divide(at_y, ex)
+    far_x = jnp.where(second, ex + far_x, far_x - REACH)
+    far_y = jnp.where(second, ey + far_y, far_y - REACH)
+    fill(outer, *divide(r, ey), jnp.where(in_x, far_x, near_x), jnp.where(in_x, near_y, far_y))
+    r, c = grid((2 * along_y, points))
+    below = r < along_y
+    y, x = divide(jnp.where(below, r, r - along_y), ex)
+    y = jnp.where(below, y + (ey - REACH), y)
+    select[...] = jnp.where(c == x * ey + y, 1.0, 0.0).astype(select.dtype)
 
 
 def kernel(
     bands, doms, ex, ey,
-    orb_hbm, rot_hbm, centre_ref, own_ref, outer_ref, select_ref, out_hbm,
-    orb, rot, halo, packed, part, code, lhs, result,
+    orb_hbm, rot_hbm, potential_hbm, out_hbm,
+    orb, rot, potential, own_ref, outer_ref, select_ref, halo, packed, part, code, lhs, result,
     load_sem, halo_send, halo_recv, code_send, code_recv, forward_send, out_sem,
 ):
     planes = part.shape[0]
@@ -85,7 +111,8 @@
     load_orb = pltpu.make_async_copy(orb_hbm, orb, load_sem.at[0])
     load_rot = pltpu.make_async_copy(rot_hbm, rot, load_sem.at[1])
     load_orb.start()
-    load_rot.start()
+    load_potential = pltpu.make_async_copy(potential_hbm, potential, load_sem.at[2])
+    load_potential.start()
 
     barrier = pltpu.get_barrier_semaphore()
     for k in range(4):
@@ -103,6 +130,7 @@
             halo[:, starts[k] : starts[k] + sizes[k], :] = jnp.zeros(
                 (planes, sizes[k], cols), halo.dtype
             )
+    fill_matrices(own_ref, outer_ref, select_ref, ex, ey)
     load_orb.wait()
     there = peers
     for k in range(4):
@@ -138,27 +166,48 @@
             device_id_type=MESH,
         )
 
-    @pl.loop(0, planes)
-    def _(p):
-        for k in (0, 1):
+    def send_halos(p, slots):
+        for k in slots:
             @pl.when(sends(k))
             def _():
                 halo_copy(k, p).start()
+
+    ahead = min(AHEAD, planes)
+    for p in range(ahead):
+        send_halos(p, (0, 1))
+    load_rot.start()
+
+    @pl.loop(0, planes)
+    def _(p):
         for n in range(0, cols, step):
             packed[p, :, n : n + step] = jnp.dot(
                 select_ref[...], orb[REACH + p, :, n : n + step],
                 preferred_element_type=jnp.float32,
             ).astype(packed.dtype)
-        for k in (2, 3):
-            @pl.when(sends(k))
-            def _():
-                halo_copy(k, p).start()
+
+        @pl.when(p < ahead)
+        def _():
+            send_halos(p, (2, 3))
+
+    load_potential.wait()
+    eye = lax.broadcasted_iota(jnp.int32, (ey, ey), 0) == lax.broadcasted_iota(
+        jnp.int32, (ey, ey), 1
+    )
+
+    def centre_weight(p):
+        rows = []
+        for x in range(ex):
+            spread = jnp.broadcast_to(potential[p, x : x + 1, :], (ey, ey))
+            rows.append(jnp.sum(jnp.where(eye, spread, 0.0), axis=1, keepdims=True))
+        value = jnp.concatenate(rows, axis=0) - centre_shift
+        return (3.0 * stencil_weights[0] * -0.5 * inverse_spacing + value) * (1.0 / spread_scale)
 
     def three_sum(value):
         return value[:points] + value[points : 2 * points] + value[2 * points :]
 
     @pl.loop(0, planes)
     def _(p):
+        centre = centre_weight(p)
         for n in range(0, cols, step):
             at = slice(n, n + step)
             total = three_sum(
@@ -170,7 +219,7 @@
                 pair = orb[REACH + p + k, :, at].astype(jnp.float32)
                 pair = pair + orb[REACH + p - k, :, at].astype(jnp.float32)
                 total = total + (FACTOR * stencil_weights[k]) * pair
-            total = total + centre_ref[p, :, 0:1] * orb[REACH + p, :, at].astype(jnp.float32)
+            total = total + centre * orb[REACH + p, :, at].astype(jnp.float32)
             part[p, :, at] = total
 
     load_rot.wait()
@@ -180,6 +229,11 @@
             @pl.when(has[k])
             def _():
                 halo_copy(k, p).wait_recv()
+
+        @pl.when(p + ahead < planes)
+        def _():
+            send_halos(p + ahead, range(4))
+
         largest = jnp.zeros((points, 1), jnp.float32)
         for n in range(0, cols, step):
             at = slice(n, n + step)
@@ -244,13 +298,13 @@
 
     @pl.loop(0, planes + 2)
     def _(p):
+        @pl.when(p >= 2)
+        def _():
+            rotate(p - 2)
+
         @pl.when(p < planes)
         def _():
             filter_plane(p)
-
-        @pl.when(p >= 2)
-        def _():
-            rotate(p - 2)
 
         @pl.when(jnp.logical_and(p >= 1, p <= planes))
         def _():
@@ -275,30 +329,29 @@
     points = ex * ey
     new_cols = rotation.shape[1]
     bands, doms = lax.axis_size("band"), lax.axis_size("dom")
-    own, outer, select = plane_matrices(ex, ey)
-    centre = (
-        3.0 * stencil_weights[0] * -0.5 * inverse_spacing
-        + (potential.reshape(planes, points, 1) - centre_shift)
-    ) / spread_scale
+    halo_rows = 2 * REACH * (ex + ey)
     bf16, f32 = jnp.bfloat16, jnp.float32
     dma = pltpu.SemaphoreType.DMA
-    whole = pl.BlockSpec(memory_space=pltpu.VMEM)
     away = pl.BlockSpec(memory_space=pl.ANY)
     result = pl.pallas_call(
         functools.partial(kernel, bands, doms, ex, ey),
         out_shape=jax.ShapeDtypeStruct((planes, points, new_cols), f32),
-        in_specs=[away, away, whole, whole, whole, whole],
+        in_specs=[away, away, away],
         out_specs=away,
         scratch_shapes=[
             pltpu.VMEM((ghosted, points, cols), bf16),
             pltpu.VMEM(rotation.shape, bf16),
-            pltpu.VMEM((planes, outer.shape[1], cols), bf16),
-            pltpu.VMEM((planes, select.shape[0], cols), bf16),
+            pltpu.VMEM((planes, ex, ey), f32),
+            pltpu.VMEM((3 * points, points), bf16),
+            pltpu.VMEM((3 * points, halo_rows), bf16),
+            pltpu.VMEM((2 * REACH * ex, points), bf16),
+            pltpu.VMEM((planes, halo_rows, cols), bf16),
+            pltpu.VMEM((planes, 2 * REACH * ex, cols), bf16),
             pltpu.VMEM((planes, points, cols), f32),
             pltpu.VMEM((bands, planes, points, cols + LANES), bf16),
             pltpu.VMEM((bands, 2 * points, cols), bf16),
             pltpu.VMEM((planes, points, new_cols), f32),
-            dma((2,)),
+            dma((3,)),
             dma((4, planes)),
             dma((4, planes)),
             dma((bands // 2, planes)),
@@ -317,10 +370,7 @@
     )(
         orbitals.reshape(ghosted, points, cols),
         rotation,
-        centre,
-        three_parts(own),
-        three_parts(outer),
-        jnp.asarray(select, bf16),
+        potential.reshape(planes, ex, ey),
     )
     return result.reshape(planes, 1, ex, ey, new_cols)
 

time: 61.1 us -> 53.7 us (0.88)
  Pallas kernels: 56.1 us -> 51.4 us
  local copies, waits for them, and re-layouts: 3.87 us -> 2.08 us
  other arithmetic: 0.76 us -> 0 us
    pallas_call x1, Pallas kernels: 56.1 us -> 51.4 us  [on_device(): pl.pallas_call(functools.partial(kernel, bands, doms, ex, ey), out_shape=...]
    unnamed x7 -> x3, local copies, waits for them, and re-layouts: 3.74 us -> 2.08 us
    div x1 -> x0, other arithmetic: 0.76 us -> none  [on_device(): (3.0 * stencil_weights[0] * -0.5 * inverse_spacing + (potential.reshape(p...]
where the time goes in v2:
time: 53.7 us; the launch traced here: 53.5 us
  Pallas kernels  51.4 us (96%)
  local copies, waits for them, and re-layouts  2.08 us (4%)
    pallas_call x1, Pallas kernels, on_device(): pl.pallas_call(functools.partial(kernel, bands, doms, ex, ey), out_shape=...  51.4 us
    unnamed x3, local copies, waits for them, and re-layouts  2.08 us

profile of v2, /device:TPU:5, one launch (start us, length us, event | category | flops | bytes accessed | tf_op | source)
XLA Modules:
  0.0 53.5 jit_solution(15219437085848169092)
XLA Ops:
  0.0 0.0 copy-start
  0.0 0.8 %copy-done = f32[8,1,8,8]{3,2,1,0:T(8,128)S(1)} copy-done((f32[8,1,8,8]{3,2,1,0:T(8,128)S(1)}, f32[8,1,8,8]{3,2,1,0:T(8,128)}, u32[]{:S(2)}) %copy-start) | copy-done | bytes 2072
  0.8 51.4 %shard_map.37 = f32[8,64,1024]{2,1,0:T(8,128)S(1)} custom-call(bf16[20,64,1024]{2,1,0:T(8,128)(2,1)} %bitcast.7, bf16[4096,1024]{1,0:T(8,128)(2,1)} %rot_hbm.1, f32[8,8,8]{2,1,0:T(8,128)S(1)} %bitcast.6), custom_call_target="tpu_custom_call" | custom-call | flops 8589934592 | bytes 13107200 | tf_op jit(solution)/shard_map/pallas_call | solution.py:336
  52.2 1.3 %copy.6 = f32[8,1,8,8,1024]{4,3,2,1,0:T(8,128)} copy(f32[8,1,8,8,1024]{4,3,2,1,0:T(8,128)S(1)} %bitcast.5) | data formatting | bytes 4194304
Async XLA Ops:
  0.0 0.8 %copy-start = (f32[8,1,8,8]{3,2,1,0:T(8,128)S(1)}, f32[8,1,8,8]{3,2,1,0:T(8,128)}, u32[]{:S(2)}) copy-start(f32[8,1,8,8]{3,2,1,0:T(8,128)} %param.5) | copy-start | bytes 6148
